TPU v7x, 32 devices: a whole 2x2x4 slice. The times are simulated.
32 devices in a mesh: row: 8 (over y, x, core), col: 4 (over z).
Axes of the slice: x: 2, y: 2, z: 4, core: 2. Of those that a mesh axis runs over, the one named last changes fastest.
Arguments:
- retarded: bfloat16 [64, 64, 64, 128], P('row', 'col'), may hold values from -4 to 4
- mirrored: bfloat16 [64, 64, 64, 128], P('col', 'row'), may hold values from -4 to 4
- lesser_panel: bfloat16 [64, 64, 16, 128], P(('col', 'row')), may hold values from -6 to 6
- initial: float32 [64, 16, 128], P(None, 'col'), may hold values from -6 to 6
- retention: float32 [64, 64], P('row'), may hold values from 0.4 to 1, as said below
- phase_angle: float32 [64], replicated, may hold values from -3.140625 to 3.140625
Outputs:
- propagated: float32 [64, 64, 16, 128], P('row', None, 'col')
Inputs may be any that keep to these rules, and one draw needn't show every extreme that they name: `retention`: each entry is the share of an orbital's amplitude kept over one step.
All inputs are finite; a program needn't handle non-finite values.
Results may differ from a plain program's by a relative error of at most 0.0026.
Values may be sent and summed in bfloat16 or wider, within the bound.
A program may use at most 128 MiB of HBM per device.

v0:
```python
import math

import jax
import jax.numpy as jnp
from jax import lax
from jax.sharding import PartitionSpec as P


def prefix(part, axis, combine, identity):
    place = lax.axis_index(axis)
    gathered = jax.tree.map(lambda a: lax.all_gather(a, axis), part)
    state = jax.tree.map(lambda a, e: jnp.zeros_like(a) + jnp.asarray(e, a.dtype), part, identity)

    def one(hop, state):
        return combine(
            state, jax.tree.map(lambda a: lax.dynamic_index_in_dim(a, hop, 0, False), gathered)
        )

    return lax.fori_loop(0, place, one, state)


def complex_scale(scale_re, scale_im, current):
    orbit_count = current.shape[-1] // 2
    current_re = current[..., :orbit_count]
    current_im = current[..., orbit_count:]
    factor_re = scale_re[:, None, None]
    factor_im = scale_im[:, None, None]
    return jnp.concatenate(
        [
            factor_re * current_re - factor_im * current_im,
            factor_re * current_im + factor_im * current_re,
        ],
        axis=-1,
    )


def self_energy(retarded_tile, mirror_tile):
    orbit_count = retarded_tile.shape[-2]
    ret_re = retarded_tile[..., :orbit_count].astype(jnp.float32)
    ret_im = retarded_tile[..., orbit_count:].astype(jnp.float32)
    mirror_re = jnp.swapaxes(mirror_tile[..., :orbit_count], -1, -2).astype(jnp.float32)
    mirror_im = jnp.swapaxes(mirror_tile[..., orbit_count:], -1, -2).astype(jnp.float32)
    square_re = ret_re * ret_re - ret_im * ret_im
    square_im = 2.0 * ret_re * ret_im
    return jnp.concatenate(
        [
            square_re * mirror_re - square_im * mirror_im,
            square_re * mirror_im + square_im * mirror_re,
        ],
        axis=-1,
    )


def per_device(retarded, mirrored, lesser_panel, initial, retention, phase_angle):
    row_count = lax.axis_size("row")
    col_count = lax.axis_size("col")
    row_index = lax.axis_index("row")
    col_index = lax.axis_index("col")
    tile_rows = retarded.shape[0]
    tile_cols = retarded.shape[1]
    orbitals = retarded.shape[2]
    panels = lesser_panel.shape[2]
    panel_share = panels // col_count
    window = tile_rows * row_count
    norm_factor = 1.0 / (orbitals * math.sqrt(window))
    gathered = lax.all_gather(lesser_panel, "row", axis=0, tiled=True)
    energy = self_energy(retarded, jnp.swapaxes(mirrored, 0, 1))
    time_labels = row_index * tile_rows + jnp.arange(tile_rows, dtype=jnp.int32)
    sources = col_index * tile_cols + jnp.arange(tile_cols, dtype=jnp.int32)
    causal = sources[None, :] <= time_labels[:, None]
    energy = jnp.where(causal[:, :, None, None], energy, 0.0).astype(jnp.bfloat16)
    energy_re = jnp.transpose(energy[..., :orbitals], (0, 2, 1, 3)).reshape(
        tile_rows * orbitals, tile_cols * orbitals
    )
    energy_im = jnp.transpose(energy[..., orbitals:], (0, 2, 1, 3)).reshape(
        tile_rows * orbitals, tile_cols * orbitals
    )
    stacked = jnp.concatenate([energy_re, energy_im], axis=0)
    panel_matrix = gathered.reshape(tile_cols * orbitals, panels * 2 * orbitals)
    product = jnp.dot(stacked, panel_matrix, preferred_element_type=jnp.float32)
    product = product.reshape(2, tile_rows, orbitals, panels, 2, orbitals)
    partial_value = (
        jnp.concatenate(
            [
                product[0, :, :, :, 0] - product[1, :, :, :, 1],
                product[0, :, :, :, 1] + product[1, :, :, :, 0],
            ],
            axis=-1,
        )
        * norm_factor
    )
    summed = lax.psum(partial_value, "col")
    integral = lax.dynamic_slice_in_dim(summed, col_index * panel_share, panel_share, 2)
    rotate_re = retention * jnp.cos(phase_angle)[None, :]
    rotate_im = retention * jnp.sin(phase_angle)[None, :]

    def advance(current, inputs):
        scale_re, scale_im, integral_step = inputs
        updated = complex_scale(scale_re, scale_im, current + integral_step)
        return (updated, updated)

    def compose(running, inputs):
        step_re, step_im = inputs
        return (
            (
                step_re * running[0] - step_im * running[1],
                step_re * running[1] + step_im * running[0],
            ),
            None,
        )

    local_end, unused = lax.scan(advance, jnp.zeros_like(initial), (rotate_re, rotate_im, integral))
    start_pair = (jnp.ones_like(phase_angle), jnp.zeros_like(phase_angle))
    (block_re, block_im), unused = lax.scan(compose, start_pair, (rotate_re, rotate_im))

    def combine(earlier, later_part):
        joined_re = later_part[0] * earlier[0] - later_part[1] * earlier[1]
        joined_im = later_part[0] * earlier[1] + later_part[1] * earlier[0]
        joined_state = complex_scale(later_part[0], later_part[1], earlier[2]) + later_part[2]
        return (joined_re, joined_im, joined_state)

    identity = (jnp.ones_like(block_re), jnp.zeros_like(block_im), jnp.zeros_like(local_end))
    prefix_re, prefix_im, prefix_state = prefix(
        (block_re, block_im, local_end), "row", combine, identity
    )
    entering = complex_scale(prefix_re, prefix_im, initial) + prefix_state
    last_state, states = lax.scan(advance, entering, (rotate_re, rotate_im, integral))
    return states


def solution(mesh):
    return jax.shard_map(
        per_device,
        mesh=mesh,
        in_specs=(
            P("row", "col", None, None),
            P("col", "row", None, None),
            P(("col", "row"), None, None, None),
            P(None, "col", None),
            P("row", None),
            P(),
        ),
        out_specs=P("row", None, "col", None),
        check_vma=False,
    )
```

profile of v0, /device:TPU:13, one launch (start us, length us, event | category | flops | bytes accessed | tf_op | source)
XLA Modules:
  0.0 284.5 jit_solution(6985331308091579528)
XLA Ops:
  7.3 5.1 %fusion.17 = (bf16[8,16,64,64]{3,2,1,0:T(8,128)(2,1)}, bf16[8,16,64,64]{3,2,1,0:T(8,128)(2,1)}) fusion(bf16[8,16,64,128]{3,2,1,0:T(8,128)(2,1)} %param.14), kind=kLoop, calls=%fused_computation.69 | loop fusion | bytes 4194304 | tf_op jit(solution)/shard_map/slice | solution.py:39
  12.5 4.2 %copy.34 = bf16[8,16,64,64]{2,3,0,1:T(8,128)(2,1)} copy(bf16[8,16,64,64]{3,2,1,0:T(8,128)(2,1)} %get-tuple-element.266) | data formatting | bytes 2097152
  16.6 4.0 %copy.35 = bf16[8,16,64,64]{2,3,0,1:T(8,128)(2,1)} copy(bf16[8,16,64,64]{3,2,1,0:T(8,128)(2,1)} %get-tuple-element.267) | data formatting | bytes 2097152
  20.7 4.2 %fusion.13 = (bf16[8,16,64,64]{2,3,0,1:T(8,128)(2,1)S(1)}, bf16[8,16,64,64]{2,3,0,1:T(8,128)(2,1)S(1)}) fusion(bf16[8,16,64,64]{2,3,0,1:T(8,128)(2,1)} %copy.35, bf16[8,16,64,64]{2,3,0,1:T(8,128)(2,1)} %copy.34, bf16[8,16,64,128]{3,2,0,1:T(8,128)(2,1)S(1)} %bitcast.111), kind=kLoop, calls=%fused_computation.53 | loop fusion | flops 8912896 | bytes 6291456 | tf_op jit(solution)/shard_map/sub | solution.py:47
  25.0 1.2 fusion.8
  26.2 3.0 %slice_bitcast_fusion.3 = (bf16[8,64,16,64]{1,3,0,2:T(8,128)(2,1)}, bf16[8,64,16,64]{1,3,0,2:T(8,128)(2,1)}) fusion(bf16[8,16,64,128]{2,3,0,1:T(8,128)(2,1)S(1)} %fusion.8), kind=kLoop, calls=%fused_computation.58 | loop fusion | bytes 4194304 | tf_op jit(solution)/shard_map/transpose | solution.py:72
  29.2 3.6 %copy.25 = bf16[8,64,16,64]{3,2,1,0:T(8,128)(2,1)S(1)} copy(bf16[8,64,16,64]{1,3,0,2:T(8,128)(2,1)} %get-tuple-element.264) | data formatting | bytes 2097152 | tf_op jit(solution)/shard_map/transpose | solution.py:72
  32.8 1.5 reshape.65
  34.3 3.6 %copy.26 = bf16[8,64,16,64]{3,2,1,0:T(8,128)(2,1)S(1)} copy(bf16[8,64,16,64]{1,3,0,2:T(8,128)(2,1)} %get-tuple-element.265) | data formatting | bytes 2097152 | tf_op jit(solution)/shard_map/transpose | solution.py:75
  37.9 2.3 reshape.66
  40.2 1.4 pad_maximum_fusion.2
  41.6 5.7 %all-gather.6.cloned.1.call-done = bf16[16,64,16,128]{3,2,1,0:T(8,128)(2,1)} async-done(((bf16[2,64,16,128]{3,2,1,0:T(8,128)(2,1)}), bf16[16,64,16,128]{3,2,1,0:T(8,128)(2,1)}) %all-gather.6.cloned.1.call-update) | async-done | bytes 4194320 | tf_op jit(solution)/shard_map/all_gather | solution.py:66
  47.4 6.3 %copy.40 = bf16[128,8,16,128]{3,1,2,0:T(8,128)(2,1)} copy(bf16[128,8,16,128]{3,2,1,0:T(8,128)(2,1)} %bitcast.112) | data formatting | bytes 8388608
  53.7 6.4 %copy.27 = bf16[1024,2048]{0,1:T(8,128)(2,1)} copy(bf16[1024,2048]{1,0:T(8,128)(2,1)} %bitcast.110) | data formatting | bytes 8388608 | tf_op jit(solution)/shard_map/reshape | solution.py:79
  60.1 10.9 %fusion.19 = f32[2,8,64,16,2,64]{5,2,4,3,1,0:T(8,128)S(1)} fusion(bf16[2,8,64,1024,1,1]{3,2,5,4,1,0:T(8,128)(2,1)S(1)} %bitcast.114, bf16[16,2,64,1024,1,1]{3,2,1,0,5,4:T(8,128)(2,1)} %bitcast.113), kind=kOutput, calls=%fused_computation.71 | convolution fusion | flops 4294967296 | bytes 14680064 | tf_op jit(solution)/shard_map/dot_general | solution.py:80
  71.0 1.4 fusion.10
  72.3 1.4 fusion.12
  73.7 3.2 %maximum_multiply_fusion = f32[8,64,16,128]{3,1,2,0:T(8,128)} fusion(f32[8,64,16,64]{3,1,2,0:T(8,128)S(1)} %fusion.10, f32[8,64,16,64]{3,1,2,0:T(8,128)S(1)} %fusion.12), kind=kLoop, calls=%fused_computation.50 | loop fusion | flops 2097152 | bytes 8388608 | tf_op jit(solution)/shard_map/mul | solution.py:83
  77.6 152.3 %all-reduce.5.cloned.1.call-done = f32[8,64,16,128]{3,1,2,0:T(8,128)} async-done(((f32[8,64,16,128]{3,1,2,0:T(8,128)}), f32[8,64,16,128]{3,1,2,0:T(8,128)}) %all-reduce.5.cloned.1.call-update) | async-done | bytes 4194320 | tf_op jit(solution)/shard_map/psum | solution.py:92
  229.9 1.3 constant_dynamic-slice_fusion.8
  231.9 4.0 %while.49 = (s32[]{:T(128)}, f32[64,4,128]{2,1,0:T(4,128)S(1)}, f32[8,64]{1,0:T(8,128)S(1)}, f32[8,64,4,128]{3,2,1,0:T(4,128)S(1)}, f32[8,64]{1,0:T(8,128)S(1)}, /*index=5*/s32[]{:T(128)}) while((s32[]{:T(128)}, f32[64,4,128]{2,1,0:T(4,128)S(1)}, f32[8,64]{1,0:T(8,128)S(1)}, f32[8,64,4,128]{3,2,1,0:T(4,128)S(1)}, f32[8,64]{1,0:T(8,128)S(1)}, ...), condition=%wide.region_4.5_spmd, body=%wide.region_3.4_spmd.sunk | while | flops 163842 | bytes 919117 | solution.py:112
  238.6 11.8 %all-reduce.2 = (f32[512]{0:T(512)S(1)}, f32[512]{0:T(512)S(1)}) all-reduce(f32[512]{0:T(512)S(1)} %dynamic-update-slice, f32[512]{0:T(512)S(1)} %dynamic-update-slice.1), channel_id=2, replica_groups=mesh['row'=8,'col'=4] {'row'}, use_global_device_ids=true, to_apply=%add | all-reduce | flops 1024 | bytes 8192
  250.6 10.9 %all-gather.8.cloned.1.call-done = f32[512,4,128]{2,1,0:T(4,128)} async-done(((f32[64,4,128]{2,1,0:T(4,128)}), f32[512,4,128]{2,1,0:T(4,128)}) %all-gather.8.cloned.1.call-update) | async-done | bytes 1048592 | tf_op jit(solution)/shard_map/all_gather | solution.py:11
  261.5 7.0 %while.50 = (s32[]{:T(128)}, f32[64]{0:T(128)S(1)}, f32[64]{0:T(128)S(1)}, f32[64,4,128]{2,1,0:T(4,128)S(1)}, s32[]{:T(128)}, /*index=5*/f32[8,64]{1,0:T(8,128)S...) while((s32[]{:T(128)}, f32[64]{0:T(128)S(1)}, ...), condition=%wide.region_6.7_spmd, body=%wide.region_5.6_spmd.sunk | while | flops 164229 | bytes 659607 | solution.py:19
  261.9 1.0 maximum_add_fusion.3
  263.2 1.0 maximum_add_fusion.3
  264.6 1.0 maximum_add_fusion.3
  266.0 1.0 maximum_add_fusion.3
  267.4 1.0 maximum_add_fusion.3
  268.9 9.0 %while.51 = (s32[]{:T(128)}, f32[64,4,128]{2,1,0:T(4,128)S(1)}, f32[8,64,4,128]{3,2,1,0:T(4,128)}, f32[8,64]{1,0:T(8,128)S(1)}, f32[8,64,4,128]{3,2,1,0:T(4,128)S(1)}, /*index=5*/f32[8,64]{1,0:T(8,128)S(1)}, s32[]{:T(128)}) while((s32[]{:T(128)}, f32[64,4,128]{2,1,0:T(4,128)S(1)}, f32[8,64,4,128]{3,2,1,0:T(4,128)}, f32[8,64]{1,0:T(8,128)S(1)}, ...), condition=%wide.region_8.9_spmd, body=%wide.region_7.8_spmd.sunk | while | flops 163842 | bytes 1050709 | solution.py:127
  271.5 0.8 bitcast_dynamic-update-slice_fusion.2
  272.7 0.8 bitcast_dynamic-update-slice_fusion.2
  (131 shorter events, 17.4 us)
Async XLA Ops:
  6.5 40.8 %all-gather.6.cloned.1.call-start = ((), (), s32[]{:S(2)}) async-start(), calls=%async_computation | async-start | bytes 4718592 | tf_op jit(solution)/shard_map/all_gather | solution.py:66
  7.3 222.6 %all-reduce.5.cloned.1.call-start = ((), (), s32[]{:S(2)}) async-start(), calls=%async_computation.1 | async-start | bytes 8388608 | tf_op jit(solution)/shard_map/psum | solution.py:92
  12.5 8.3 %copy-start = (bf16[16,8,64,128]{3,2,1,0:T(8,128)(2,1)S(1)}, bf16[16,8,64,128]{3,2,1,0:T(8,128)(2,1)}, u32[]{:S(2)}) copy-start(bf16[16,8,64,128]{3,2,1,0:T(8,128)(2,1)} %param.15) | copy-start | bytes 6291460
  76.9 0.7 copy-start.4
  76.9 0.7 copy-start.3
  76.9 184.6 %all-gather.8.cloned.1.call-start = ((), (), s32[]{:S(2)}) async-start(), calls=%async_computation.2 | async-start | bytes 1179648 | tf_op jit(solution)/shard_map/all_gather | solution.py:11
  231.2 5.4 %copy-start.5 = (u32[32]{0:T(128)S(1)}, u32[32]{0:T(128)}, u32[]{:S(2)}) copy-start(u32[32]{0:T(128)} %constant.72) | copy-start | bytes 388
  235.9 0.6 copy-start.1
  235.9 32.7 %copy-start.2 = (f32[64,4,128]{2,1,0:T(4,128)S(1)}, f32[64,4,128]{2,1,0:T(4,128)}, u32[]{:S(2)}) copy-start(f32[64,4,128]{2,1,0:T(4,128)} %param.17) | copy-start | bytes 393220
Sparse Core Ops, SparseCore 0:
  9.2 38.0 all-gather.5
  77.0 152.8 all-reduce.4
  236.7 24.7 all-gather.7
where the time goes:
time: 287 us; the launch traced here: 284 us
  waiting for transfers between devices  170 us (59%)
  local copies, waits for them, and re-layouts  44.7 us (16%)
  other arithmetic  32.5 us (11%)
  between operations  14 us (5%)
  blocking collectives  11.8 us (4%)
  matrix products  10.9 us (4%)
    psum x1, waiting for transfers between devices, per_device(): summed = lax.psum(partial_value, 'col')  152 us
    unnamed x20, local copies, waits for them, and re-layouts  16.8 us
    unnamed x1, blocking collectives  11.8 us
    all_gather x1, waiting for transfers between devices, prefix(): gathered = jax.tree.map(lambda a: lax.all_gather(a, axis), part)  10.9 us
    dot_general x1, matrix products, per_device(): product = jnp.dot(stacked, panel_matrix, preferred_element_type=jnp.float32)  10.9 us
    transpose x2, local copies, waits for them, and re-layouts, per_device(): jnp.transpose(energy[..., :orbitals], (0, 2, 1, 3))  6.62 us
    dynamic_update_slice x8, other arithmetic, per_device(): lax.scan(advance, entering, (rotate_re, rotate_im, integral))  6.41 us
    reshape x1, local copies, waits for them, and re-layouts, per_device(): panel_matrix = gathered.reshape(tile_cols * orbitals, panels * 2 * orbitals)  6.39 us
  transfers between devices with their start and end apart: 3, of which 3 were waited for; matrix products, arithmetic and copies ran while one was open for 13% of the time, Pallas kernels for 0%

commit v1 on v0

v1 whole, which is shorter than its diff:
```python
import functools
import math

import jax
import jax.numpy as jnp
from jax import lax
from jax.experimental import pallas as pl
from jax.experimental.pallas import tpu as pltpu
from jax.sharding import PartitionSpec as P

MESH = pl.DeviceIdType.MESH


def kernel(
    NR, NC, TR, TC, O, PS, norm,
    ret, mir, lp, init, fre, fim, rprod, cpow,
    out,
    E, L, acc, tmp, zl, zr, zs, ends, end_out, rp,
    ls, lf, lr, zsend, zrecv_l, zrecv_r, es, er, rs, rr,
):
    r = lax.axis_index("row")
    c = lax.axis_index("col")
    half = lax.rem(r, 2)
    k = r // 2
    pairs = NR // 2
    partner = r + 1 - 2 * half
    last_time = (k + 1) * 2 * TR - 1
    act = c * TC <= last_time
    act_right = jnp.logical_and(c + 1 < NC, (c + 1) * TC <= last_time)
    has_left = c > 0
    n_up = NC - 1 - c

    bar = pltpu.get_barrier_semaphore()

    def greet(j, carry):
        pl.semaphore_signal(bar, inc=1, device_id=(lax.rem(r + j, NR), c), device_id_type=MESH)
        return carry

    lax.fori_loop(1, NR, greet, 0)

    @pl.when(has_left)
    def _():
        pl.semaphore_signal(bar, inc=1, device_id=(r, c - 1), device_id_type=MESH)

    @pl.when(c < NC - 1)
    def _():
        pl.semaphore_signal(bar, inc=1, device_id=(r, c + 1), device_id_type=MESH)

    for q in range(NC):
        L[q, :, r] = lp[q]

    pl.semaphore_wait(
        bar, NR - 1 + jnp.where(has_left, 1, 0) + jnp.where(c < NC - 1, 1, 0)
    )

    def share(i):
        return jnp.where(i < n_up, NC - 1 - i, jnp.where(i < NC - 1, i - n_up, c))

    def row_act(j):
        return c * TC <= (j + 1) * 2 * TR - 1

    def l_direct(i, j):
        q = share(i)
        return pltpu.make_async_remote_copy(
            src_ref=L.at[q, :, r], dst_ref=L.at[q, :, r],
            send_sem=ls.at[i, j], recv_sem=lr.at[i, r],
            device_id=(2 * j + half, c), device_id_type=MESH,
        )

    def l_forward(i, j):
        q = share(i)
        s = 2 * j + half
        return pltpu.make_async_remote_copy(
            src_ref=L.at[q, :, s], dst_ref=L.at[q, :, s],
            send_sem=lf.at[i, j], recv_sem=lr.at[i, s],
            device_id=(partner, c), device_id_type=MESH,
        )

    def l_arrived(i, s):
        q = share(i)
        return pltpu.make_async_remote_copy(
            src_ref=L.at[q, :, s], dst_ref=L.at[q, :, s],
            send_sem=lf.at[i, 0], recv_sem=lr.at[i, s],
            device_id=(partner, c), device_id_type=MESH,
        )

    def others(fn):
        def body(j, carry):
            @pl.when(jnp.logical_and(j != k, row_act(j)))
            def _():
                fn(j)
            return carry

        lax.fori_loop(0, pairs, body, 0)

    def send_share(i, carry):
        others(lambda j: l_direct(i, j).start())

        @pl.when(act)
        def _():
            l_forward(i, k).start()

        return carry

    lax.fori_loop(0, NC, send_share, 0)

    def r_copy(target):
        return pltpu.make_async_remote_copy(
            src_ref=rprod, dst_ref=rp.at[r],
            send_sem=rs.at[target], recv_sem=rr.at[r],
            device_id=(target, c), device_id_type=MESH,
        )

    def later(fn):
        def body(t, carry):
            fn(t)
            return carry

        lax.fori_loop(r + 1, NR, body, 0)

    later(lambda t: r_copy(t).start())

    lane = lax.broadcasted_iota(jnp.int32, (O, 2 * O), 1)
    low = lane < O
    upper = jnp.where(low, 0, 1)

    @pl.when(act)
    def _():
        def energy(t, carry):
            room = r * TR + t - c * TC
            for s2 in range(TC // 2):
                a0 = ret[t, 2 * s2].astype(jnp.float32)
                a1 = ret[t, 2 * s2 + 1].astype(jnp.float32)
                ar = jnp.where(low, a0, pltpu.roll(a1, O, 1))
                ai = jnp.where(low, pltpu.roll(a0, O, 1), a1)
                m = jnp.concatenate([mir[2 * s2, t], mir[2 * s2 + 1, t]], axis=0)
                mt = m.astype(jnp.float32).T
                mr, mi = mt[:O], mt[O:]
                sr = ar * ar - ai * ai
                si = 2.0 * ar * ai
                keep = upper + 2 * s2 <= room
                e_re = jnp.where(keep, sr * mr - si * mi, 0.0)
                e_im = jnp.where(keep, sr * mi + si * mr, 0.0)
                E[t, 0, :, s2 * 2 * O:(s2 + 1) * 2 * O] = e_re.astype(jnp.bfloat16)
                E[t, 1, :, s2 * 2 * O:(s2 + 1) * 2 * O] = e_im.astype(jnp.bfloat16)
            return carry

        lax.fori_loop(0, TR, energy, 0)

    sign = jnp.where(low, -1.0, 1.0).astype(jnp.float32)

    def z_up(q, p, src):
        return pltpu.make_async_remote_copy(
            src_ref=src.at[q, p], dst_ref=zl.at[q, p],
            send_sem=zsend.at[q, p], recv_sem=zrecv_l.at[q, p],
            device_id=(r, c + 1), device_id_type=MESH,
        )

    def z_down(q, p, src):
        return pltpu.make_async_remote_copy(
            src_ref=src.at[q, p], dst_ref=zr.at[q, p],
            send_sem=zsend.at[q, p], recv_sem=zrecv_r.at[q, p],
            device_id=(r, c - 1), device_id_type=MESH,
        )

    def end_copy(p, target):
        return pltpu.make_async_remote_copy(
            src_ref=end_out.at[p], dst_ref=ends.at[r, p],
            send_sem=es.at[p, target], recv_sem=er.at[p, r],
            device_id=(target, c), device_id_type=MESH,
        )

    def combine(h):
        for t in range(TR):
            a = acc[t, 0, :, h * 2 * O:(h + 1) * 2 * O]
            b = acc[t, 1, :, h * 2 * O:(h + 1) * 2 * O]
            tmp[h, t] = (a + sign * pltpu.roll(b, O, 1)) * norm

    def one_share(i, carry):
        q = share(i)

        @pl.when(act)
        def _():
            def pass_on(j, carry):
                @pl.when(j != k)
                def _():
                    l_arrived(i, 2 * j + half).wait_recv()
                    l_forward(i, j).start()
                return carry

            lax.fori_loop(0, pairs, pass_on, 0)

            def from_partner(j, carry):
                l_arrived(i, 2 * j + 1 - half).wait_recv()
                return carry

            lax.fori_loop(0, pairs, from_partner, 0)

        def one_pair(pp, carry):
            @pl.when(act)
            def _():
                depth = TC * O
                rhs = jnp.concatenate(
                    [L[q, 2 * pp].reshape(depth, 2 * O), L[q, 2 * pp + 1].reshape(depth, 2 * O)],
                    axis=1,
                )
                lhs = E[...].reshape(TR * 2 * O, depth)
                acc[...] = jnp.dot(lhs, rhs, preferred_element_type=jnp.float32).reshape(
                    TR, 2, O, 4 * O
                )

            for h in range(2):
                p = 2 * pp + h

                @pl.when(act)
                def _():
                    combine(h)

                @pl.when(jnp.logical_and(i < n_up, has_left))
                def _():
                    z_up(q, p, zs).wait_recv()

                    @pl.when(act)
                    def _():
                        tmp[h] += zl[q, p].astype(jnp.float32)

                @pl.when(jnp.logical_and(i < n_up, act))
                def _():
                    zs[q, p] = tmp[h].astype(jnp.bfloat16)
                    z_up(q, p, zs).start()

                @pl.when(jnp.logical_and(i < n_up, jnp.logical_not(act)))
                def _():
                    z_up(q, p, zl).start()

                @pl.when(jnp.logical_and(jnp.logical_and(i >= n_up, i < NC - 1), act))
                def _():
                    @pl.when(act_right)
                    def _():
                        z_down(q, p, zs).wait_recv()
                        tmp[h] += zr[q, p].astype(jnp.float32)

                    zs[q, p] = tmp[h].astype(jnp.bfloat16)
                    z_down(q, p, zs).start()

                @pl.when(i == NC - 1)
                def _():
                    @pl.when(jnp.logical_not(act))
                    def _():
                        tmp[h] = jnp.zeros_like(tmp[h])

                    @pl.when(has_left)
                    def _():
                        z_up(q, p, zs).wait_recv()
                        tmp[h] += zl[q, p].astype(jnp.float32)

                    @pl.when(act_right)
                    def _():
                        z_down(q, p, zs).wait_recv()
                        tmp[h] += zr[q, p].astype(jnp.float32)

                    x = jnp.zeros((O, 2 * O), jnp.float32)
                    for t in range(TR):
                        v = tmp[h, t]
                        out[p, t] = v
                        x = x + v
                        x = fre[t] * x + fim[t] * pltpu.roll(x, O, 1)
                    end_out[p] = x
                    later(lambda target: end_copy(p, target).start())

            return carry

        return lax.fori_loop(0, PS // 2, one_pair, carry)

    lax.fori_loop(0, NC, one_share, 0)

    def r_arrive(s, carry):
        pltpu.make_async_remote_copy(
            src_ref=rprod, dst_ref=rp.at[s],
            send_sem=rs.at[0], recv_sem=rr.at[s],
            device_id=(partner, c), device_id_type=MESH,
        ).wait_recv()
        return carry

    lax.fori_loop(0, r, r_arrive, 0)

    def finish(p, carry):
        def enter(s, x):
            pltpu.make_async_remote_copy(
                src_ref=end_out.at[p], dst_ref=ends.at[s, p],
                send_sem=es.at[p, 0], recv_sem=er.at[p, s],
                device_id=(partner, c), device_id_type=MESH,
            ).wait_recv()
            kept = jnp.broadcast_to(rp[s, 0:1, :], (2 * O, 2 * O)).T[:O]
            turned = cpow[0] * x + cpow[1] * pltpu.roll(x, O, 1)
            return kept * turned + ends[s, p]

        x = lax.fori_loop(0, r, enter, init[p])
        for t in range(TR):
            x = x + out[p, t]
            x = fre[t] * x + fim[t] * pltpu.roll(x, O, 1)
            out[p, t] = x
        return carry

    lax.fori_loop(0, PS, finish, 0)

    later(lambda t: r_copy(t).wait_send())

    def drain_share(i, carry):
        q = share(i)
        others(lambda j: l_direct(i, j).wait_send())

        @pl.when(act)
        def _():
            def one(j, carry):
                l_forward(i, j).wait_send()
                return carry

            lax.fori_loop(0, pairs, one, 0)

        def z_one(p, carry):
            @pl.when(i < n_up)
            def _():
                z_up(q, p, zs).wait_send()

            @pl.when(jnp.logical_and(jnp.logical_and(i >= n_up, i < NC - 1), act))
            def _():
                z_down(q, p, zs).wait_send()

            return carry

        lax.fori_loop(0, PS, z_one, 0)
        return carry

    lax.fori_loop(0, NC, drain_share, 0)

    def drain_end(p, carry):
        later(lambda t: end_copy(p, t).wait_send())
        return carry

    lax.fori_loop(0, PS, drain_end, 0)


def per_device(retarded, mirrored, lesser_panel, initial, retention, phase_angle):
    NR = lax.axis_size("row")
    NC = lax.axis_size("col")
    TR, TC, O = retarded.shape[0], retarded.shape[1], retarded.shape[2]
    S2, PN = lesser_panel.shape[0], lesser_panel.shape[2]
    PS = PN // NC
    SK = S2 * O
    norm = 1.0 / (O * math.sqrt(TR * NR))
    lp = jnp.transpose(lesser_panel, (2, 0, 1, 3)).reshape(NC, PS, SK, 2 * O)
    init = jnp.transpose(initial, (1, 0, 2))
    cos, sin = jnp.cos(phase_angle), jnp.sin(phase_angle)
    sign = jnp.concatenate([-jnp.ones((O,), jnp.float32), jnp.ones((O,), jnp.float32)])
    fre = jnp.broadcast_to((retention * cos)[:, :, None], (TR, O, 2 * O))
    fim = (retention * sin)[:, :, None] * sign
    pow_re, pow_im = cos, sin
    kept = retention[0]
    for t in range(1, TR):
        pow_re, pow_im = pow_re * cos - pow_im * sin, pow_re * sin + pow_im * cos
        kept = kept * retention[t]
    cpow = jnp.stack(
        [jnp.broadcast_to(pow_re[:, None], (O, 2 * O)), pow_im[:, None] * sign]
    )
    rprod = jnp.broadcast_to(jnp.concatenate([kept, kept])[None], (8, 2 * O))
    f32, bf16 = jnp.float32, jnp.bfloat16
    dma = pltpu.SemaphoreType.DMA
    states = pl.pallas_call(
        functools.partial(kernel, NR, NC, TR, TC, O, PS, norm),
        out_shape=jax.ShapeDtypeStruct((PS, TR, O, 2 * O), f32),
        in_specs=[pl.BlockSpec(memory_space=pltpu.VMEM)] * 8,
        out_specs=pl.BlockSpec(memory_space=pltpu.VMEM),
        scratch_shapes=[
            pltpu.VMEM((TR, 2, O, TC * O), bf16),
            pltpu.VMEM((NC, PS, NR, SK, 2 * O), bf16),
            pltpu.VMEM((TR, 2, O, 4 * O), f32),
            pltpu.VMEM((2, TR, O, 2 * O), f32),
            pltpu.VMEM((NC, PS, TR, O, 2 * O), bf16),
            pltpu.VMEM((NC, PS, TR, O, 2 * O), bf16),
            pltpu.VMEM((NC, PS, TR, O, 2 * O), bf16),
            pltpu.VMEM((NR, PS, O, 2 * O), f32),
            pltpu.VMEM((PS, O, 2 * O), f32),
            pltpu.VMEM((NR, 8, 2 * O), f32),
            dma((NC, NR // 2)),
            dma((NC, NR // 2)),
            dma((NC, NR)),
            dma((NC, PS)),
            dma((NC, PS)),
            dma((NC, PS)),
            dma((PS, NR)),
            dma((PS, NR)),
            dma((NR,)),
            dma((NR,)),
        ],
        compiler_params=pltpu.CompilerParams(
            collective_id=0, has_side_effects=True, vmem_limit_bytes=56 * 1024 * 1024
        ),
    )(retarded, mirrored, lp, init, fre, fim, rprod, cpow)
    return jnp.transpose(states, (1, 2, 0, 3))


def solution(mesh):
    return jax.shard_map(
        per_device,
        mesh=mesh,
        in_specs=(
            P("row", "col", None, None),
            P("col", "row", None, None),
            P(("col", "row"), None, None, None),
            P(None, "col", None),
            P("row", None),
            P(),
        ),
        out_specs=P("row", None, "col", None),
        check_vma=False,
    )
```

time: 287 us -> 85.7 us (0.30)
  waiting for transfers between devices: 170 us -> 0 us
  Pallas kernels: 0 us -> 72.1 us
  local copies, waits for them, and re-layouts: 44.7 us -> 8.61 us
  other arithmetic: 32.5 us -> 4.64 us
  between operations: 14 us -> 0.02 us
  blocking collectives: 11.8 us -> 0 us
  matrix products: 10.9 us -> 0 us
    psum x1 -> x0, waiting for transfers between devices: 152 us -> none  [per_device(): summed = lax.psum(partial_value, 'col')]
    pallas_call x0 -> x1, Pallas kernels: none -> 72.1 us  [per_device(): pl.pallas_call(functools.partial(kernel, NR, NC, TR, TC, O, PS, norm), ou...]
    all_gather x2 -> x0, waiting for transfers between devices: 16.7 us -> none  [the longest x1 10.9 us: prefix(): gathered = jax.tree.map(lambda a: lax.all_gather(a, axis), part)]
    unnamed x20 -> x1, local copies, waits for them, and re-layouts: 16.8 us -> 1.57 us
    unnamed x1 -> x0, blocking collectives: 11.8 us -> none
    sub x29 -> x1, other arithmetic: 11.6 us -> 0.02 us  [per_device(): pow_re, pow_im = (pow_re * cos - pow_im * sin, pow_re * sin + pow_im * cos)]
    dot_general x1 -> x0, matrix products: 10.9 us -> none  [per_device(): product = jnp.dot(stacked, panel_matrix, preferred_element_type=jnp.float32)]
    reshape x3 -> x0, local copies, waits for them, and re-layouts: 10.2 us -> none  [the longest x1 6.39 us: per_device(): panel_matrix = gathered.reshape(tile_cols * orbitals, panels * 2 * orbitals)]
  transfers between devices with their start and end apart: 3 -> 0, of which waited for: 3 -> 0; matrix products, arithmetic and copies ran while one was open for 13% -> 0% of each run, Pallas kernels for 0% -> 0%
where the time goes in v1:
time: 85.7 us; the launch traced here: 85.4 us
  Pallas kernels  72.1 us (84%)
  local copies, waits for them, and re-layouts  8.61 us (10%)
  other arithmetic  4.64 us (5%)
    pallas_call x1, Pallas kernels, per_device(): pl.pallas_call(functools.partial(kernel, NR, NC, TR, TC, O, PS, norm), ou...  72.1 us
    transpose x1, local copies, waits for them, and re-layouts, per_device(): return jnp.transpose(states, (1, 2, 0, 3))  2.87 us
    mul x2, other arithmetic, per_device(): fim = (retention * sin)[:, :, None] * sign  2.19 us
    transpose x1, local copies, waits for them, and re-layouts, per_device(): lp = jnp.transpose(lesser_panel, (2, 0, 1, 3)).reshape(NC, PS, SK, 2 * O)  1.97 us

profile of v1, /device:TPU:13, one launch (start us, length us, event | category | flops | bytes accessed | tf_op | source)
XLA Modules:
  0.0 85.4 jit_solution(9277393756553974656)
XLA Ops:
  0.0 1.0 %multiply_bitcast_fusion = f32[64]{0:T(128)S(1)} fusion(f32[8,64]{1,0:T(8,128)} %param.10), kind=kLoop, calls=%fused_computation.7 | loop fusion | flops 448 | bytes 2304 | tf_op jit(solution)/shard_map/mul | solution.py:362
  1.0 0.1 pad_maximum_fusion.1
  1.1 0.7 fusion
  1.8 0.6 broadcast_in_dim.5.rprod
  2.4 0.7 broadcast_multiply_fusion.2
  3.1 0.7 broadcast_multiply_fusion.1
  3.8 0.1 stack_broadcast_in_dim.2
  3.9 0.6 pad_maximum_fusion.cpow
  4.5 1.6 %copy.11 = f32[64,4,128]{2,0,1:T(8,128)} copy(f32[64,4,128]{2,1,0:T(4,128)} %param.9) | data formatting | bytes 262144 | tf_op args[3]
  6.1 1.5 %broadcast_multiply_fusion.fim = f32[8,64,128]{2,1,0:T(8,128)} fusion(f32[128]{0:T(128)} %constant.4.clone.1, f32[8,64]{1,0:T(8,128)S(1)} %get-tuple-element.8), kind=kLoop, calls=%fused_computation.1 | loop fusion | flops 65536 | bytes 264704 | tf_op jit(solution)/shard_map/mul | solution.py:357
  7.6 0.8 broadcast_in_dim.4.fre
  8.4 2.0 %copy.7 = bf16[16,2,64,128]{3,2,1,0:T(8,128)(2,1)} copy(bf16[16,2,64,128]{3,0,2,1:T(8,128)(2,1)} %bitcast.11) | data formatting | bytes 1048576 | tf_op jit(solution)/shard_map/transpose | solution.py:352
  10.4 72.1 %shard_map.64 = f32[4,8,64,128]{3,2,1,0:T(8,128)} custom-call(bf16[8,16,64,128]{3,2,1,0:T(8,128)(2,1)} %ret.1, bf16[16,8,64,128]{3,2,1,0:T(8,128)(2,1)} %mir.1, bf16[4,4,128,128]{3,2,1,0:T(8,128)(2,1)} %bitcast.9, f32[4,64,128]{2,1,0:T(8,128)} %bitcast.10, f32[8,64,128]{2,1,0:T(8,128)} %broadcast_in_dim.4.fre, f32[8,64,128]{2,1,0:T(8,128)} %broadcast_multiply_fusion.fim, ...), custom_call_target="tpu_custom_call" | custom-call | tf_op jit(solution)/shard_map/pallas_call | solution.py:369
  82.5 2.9 %copy.9 = f32[8,64,4,128]{3,2,1,0:T(4,128)} copy(f32[8,64,4,128]{3,1,0,2:T(8,128)} %bitcast.8) | data formatting | bytes 2097152 | tf_op jit(solution)/shard_map/transpose | solution.py:400
  (2 shorter events, 0.0 us)
